TPU v7x, 32 devices: a whole 2x2x4 slice. The times are simulated.
32 devices in a mesh: ctx: 8 (over y, x, core), fsdp: 4 (over z).
Axes of the slice: x: 2, y: 2, z: 4, core: 2. Of those that a mesh axis runs over, the one named last changes fastest.
Arguments:
- queries: bfloat16 [6144, 3072], P('ctx', 'fsdp'), may hold values from -120 to 120
- key_input: bfloat16 [6144, 3072], P('ctx', 'fsdp'), may hold values from -120 to 120
- value_input: bfloat16 [6144, 3072], P('ctx', 'fsdp'), may hold values from -6 to 6
- out_grad: bfloat16 [6144, 3072], P('ctx', 'fsdp'), may hold values from -21 to 21
- norm_gains: float32 [3, 128], replicated, may hold values from 0.1 to 1.9
- block_lists: int32 [48, 5], P('ctx'), may hold values from -1 to 47, as said below
Outputs:
- attended: bfloat16 [6144, 3072], P('ctx', 'fsdp')
- query_grad: bfloat16 [6144, 3072], P('ctx', 'fsdp')
- key_grad: bfloat16 [6144, 3072], P('ctx', 'fsdp')
- value_grad: bfloat16 [6144, 3072], P('ctx', 'fsdp')
- gain_grad: float32 [3, 128], replicated
Inputs may be any that keep to these rules, and one draw needn't show every extreme that they name: `block_lists`: row b holds, in this order, b, b - 1, b - 2, s and s - 3, where s = b - (b mod 3) - 1; any entry but the first may be -1 instead; an entry is -1 wherever that number would be negative, and the fourth entry is -1 wherever b mod 3 is 0 or 1.
All inputs are finite; a program needn't handle non-finite values.
Results may differ from a plain program's by a relative error of at most 0.014.
Values may be sent and summed in bfloat16 or wider, within the bound.
A program may use at most 128 MiB of HBM per device.

v0:
```python
import functools
import math

import jax
import jax.numpy as jnp
from jax import lax
from jax.experimental import pallas as pl
from jax.experimental.pallas import tpu as pltpu
from jax.sharding import PartitionSpec as P

EPS = 1e-06
B = 128
D = 128
F32 = jnp.float32
BF16 = jnp.bfloat16
MESH = pl.DeviceIdType.MESH

KEYS = (-2, -4, -1, 0, 1, 2, 3, 4, 5)
SEEN = {-2: (0, 0), -4: (0, 2), -1: (0, 5), 0: (0, 2), 1: (1, 3), 2: (2, 5), 3: (3, 5), 4: (4, 5), 5: (5, 5)}
BASE = {}
_total = 0
for _key in KEYS:
    BASE[_key] = _total
    _total += SEEN[_key][1] - SEEN[_key][0] + 1
PAIRS = _total
WINDOW = []
for _b in range(6):
    _g = _b - _b % 3
    _low = {0: -1, 3: 2}[_g]
    _far = {0: -4, 3: -1}[_g]
    if _b % 3 == 0:
        WINDOW.append(((_b - 2, 2), (_far, 4), (_low, 1), (_b, 0)))
    elif _b % 3 == 1:
        WINDOW.append(((_far, 4), (_low, 2), (_b - 1, 1), (_b, 0)))
    else:
        WINDOW.append(((_far, 4), (_low, 3), (_b - 2, 2), (_b - 1, 1), (_b, 0)))
HALO_AT = {-4: 0, -2: 1, -1: 2}
TAIL = (2, 4, 5)
PIECES = ((2 * B, 0, B), (4 * B, B, 2 * B))


def rowmean(x):
    return jnp.sum(x, axis=-1, keepdims=True) * (1.0 / D)


def fold(x):
    return jnp.sum(x.reshape(x.shape[0] // 8, 8, D), axis=0)


def dot_nt(a, b):
    return lax.dot_general(a, b, (((1,), (1,)), ((), ())), preferred_element_type=F32)


def dot_nn(a, b):
    return lax.dot_general(a, b, (((1,), (0,)), ((), ())), preferred_element_type=F32)


def kernel(
    n, m, heads, factor,
    q_hbm, k_hbm, v_hbm, do_hbm, gains, lists,
    att_hbm, dq_hbm, dk_hbm, dv_hbm, gain_out,
    q_in, k_in, v_in, do_in, halo, back, ret, tail_acc,
    att_o, dq_o, dk_o, dv_o, p_s, ds_s, dor_s, gacc, g1, g2,
    in_sem, out_sem, hs_sem, hr_sem, bs_sem, br_sem, s1, r1, s2, r2,
):
    me = lax.axis_index("ctx")
    mf = lax.axis_index("fsdp")
    ins = ((q_hbm, q_in), (k_hbm, k_in), (v_hbm, v_in), (do_hbm, do_in))
    outs = ((att_o, att_hbm), (dq_o, dq_hbm), (dk_o, dk_hbm), (dv_o, dv_hbm))

    def cols(h):
        return pl.ds(pl.multiple_of(h * D, D), D)

    def in_copy(t, h):
        return pltpu.make_async_copy(ins[t][0].at[:, cols(h)], ins[t][1].at[h], in_sem.at[t, h])

    def out_copy(t, h):
        return pltpu.make_async_copy(outs[t][0].at[h], outs[t][1].at[:, cols(h)], out_sem.at[t, h])

    def halo_copy(h, kv, piece):
        src_row, dst_row, size = PIECES[piece]
        return pltpu.make_async_remote_copy(
            src_ref=(k_hbm, v_hbm)[kv].at[pl.ds(src_row, size), cols(h)],
            dst_ref=halo.at[h, kv, pl.ds(dst_row, size)],
            send_sem=hs_sem.at[h, kv, piece],
            recv_sem=hr_sem.at[h, kv, piece],
            device_id={"ctx": me + 1},
            device_id_type=MESH,
        )

    def back_copy(h):
        return pltpu.make_async_remote_copy(
            src_ref=back.at[h],
            dst_ref=ret.at[h],
            send_sem=bs_sem.at[h],
            recv_sem=br_sem.at[h],
            device_id={"ctx": me - 1},
            device_id_type=MESH,
        )

    def load_inputs(h, c):
        for t in (1, 0, 2, 3):
            in_copy(t, h).start()
        return c

    lax.fori_loop(0, heads, load_inputs, 0)

    barrier = pltpu.get_barrier_semaphore()

    def greet_ctx(k, c):
        pl.semaphore_signal(barrier, inc=1, device_id={"ctx": lax.rem(me + k, n)}, device_id_type=MESH)
        return c

    def greet_fsdp(k, c):
        pl.semaphore_signal(barrier, inc=1, device_id={"fsdp": lax.rem(mf + k, m)}, device_id_type=MESH)
        return c

    lax.fori_loop(1, n, greet_ctx, 0)
    lax.fori_loop(1, m, greet_fsdp, 0)
    pl.semaphore_wait(barrier, n - 1 + m - 1)

    @pl.when(me < n - 1)
    def _():
        def send(h, c):
            for piece in range(2):
                for kv in range(2):
                    halo_copy(h, kv, piece).start()
            return c

        lax.fori_loop(0, heads, send, 0)

    @pl.when(me == 0)
    def _():
        halo[...] = jnp.zeros_like(halo)

    @pl.when(me == n - 1)
    def _():
        ret[...] = jnp.zeros_like(ret)

    gacc[...] = jnp.zeros_like(gacc)
    inv_root = 1.0 / math.sqrt(D)
    c2 = math.log2(math.e) * inv_root
    gq = gains[0:1, :]
    gk = gains[1:2, :]
    go = gains[2:3, :]
    gq2 = gq * c2
    row_id = lax.broadcasted_iota(jnp.int32, (B, B), 0)
    col_id = lax.broadcasted_iota(jnp.int32, (B, B), 1)
    causal = row_id >= col_id

    def key_back(raw, dkn):
        scale = lax.rsqrt(rowmean(raw * raw) + EPS)
        unit = raw * scale
        inner = dkn * gk
        return scale * (inner - unit * rowmean(inner * unit)), unit

    def finish_tail(h):
        @pl.when(me < n - 1)
        def _():
            back_copy(h).wait_recv()

        for i, blk in enumerate(TAIL):
            rows = pl.ds(blk * B, B)
            raw = k_in[h, rows, :].astype(F32)
            dkn = tail_acc[h, 0, pl.ds(i * B, B), :] + ret[h, 0, pl.ds(i * B, B), :].astype(F32)
            grad, _ = key_back(raw, dkn)
            dk_o[h, rows, :] = grad.astype(BF16)
            dvv = tail_acc[h, 1, pl.ds(i * B, B), :] + ret[h, 1, pl.ds(i * B, B), :].astype(F32)
            dv_o[h, rows, :] = dvv.astype(BF16)
        out_copy(2, h).start()
        out_copy(3, h).start()

    def head(h, c):
        for t in range(4):
            in_copy(t, h).wait()
        kr = k_in[h].astype(F32)
        kb = (kr * lax.rsqrt(rowmean(kr * kr) + EPS) * gk).astype(BF16)
        qr = q_in[h].astype(F32)
        rq = lax.rsqrt(rowmean(qr * qr) + EPS)
        qs = (qr * rq * gq2).astype(BF16)
        qt = qs.T
        vb = v_in[h]

        @pl.when(me > 0)
        def _():
            for piece in range(2):
                for kv in range(2):
                    halo_copy(h, kv, piece).wait_recv()

        hr = halo[h, 0].astype(F32)
        hn = hr * lax.rsqrt(rowmean(hr * hr) + EPS)
        hb = (hn * gk).astype(BF16)
        hv = halo[h, 1]

        def kblk(u):
            return kb[u * B:(u + 1) * B] if u >= 0 else hb[HALO_AT[u] * B:(HALO_AT[u] + 1) * B]

        def vblk(u):
            return vb[u * B:(u + 1) * B] if u >= 0 else hv[HALO_AT[u] * B:(HALO_AT[u] + 1) * B]

        ones = jnp.ones((B, D), BF16)
        for b in range(6):
            rows = slice(b * B, (b + 1) * B)
            qb = qs[rows]
            keys = jnp.concatenate([kblk(u) for u, _ in WINDOW[b]], axis=0)
            vals = jnp.concatenate([vblk(u) for u, _ in WINDOW[b]], axis=0)
            s = dot_nt(qb, keys)
            ps = []
            for i, (u, slot) in enumerate(WINDOW[b]):
                e = jnp.exp2(s[:, i * B:(i + 1) * B])
                if slot == 0:
                    e = jnp.where(causal, e, 0.0)
                else:
                    e = e * jnp.where(lists[b, slot] >= 0, 1.0, 0.0).astype(F32)
                ps.append(e)
            pb = jnp.concatenate([e.astype(BF16) for e in ps], axis=1)
            vone = jnp.concatenate(
                [vals, jnp.concatenate([ones] * len(ps), axis=0)], axis=1)
            acc = dot_nn(pb, vone)
            r = 1.0 / acc[:, D:]
            out = acc[:, :D] * r
            att_o[h, pl.ds(b * B, B), :] = (out * go).astype(BF16)
            dout = do_in[h, pl.ds(b * B, B), :].astype(F32)
            gacc[2] += fold(dout * out)
            dor = (dout * go * r).astype(BF16)
            dor_s[pl.ds(b * B, B), :] = dor
            delta = jnp.sum(dor.astype(F32) * out, axis=-1, keepdims=True)
            dp = dot_nt(dor, vals)
            dss = []
            for i, (u, slot) in enumerate(WINDOW[b]):
                ds = (ps[i] * (dp[:, i * B:(i + 1) * B] - delta)).astype(BF16)
                dss.append(ds)
                at = pl.ds((BASE[u] + b - SEEN[u][0]) * B, B)
                p_s[at, :] = pb[:, i * B:(i + 1) * B]
                ds_s[at, :] = ds
            dqn = dot_nn(jnp.concatenate(dss, axis=1), keys) * inv_root
            raw = qr[rows]
            scale = rq[rows]
            unit = raw * scale
            gacc[0] += fold(dqn * unit)
            inner = dqn * gq
            grad = scale * (inner - unit * rowmean(inner * unit))
            dq_o[h, pl.ds(b * B, B), :] = grad.astype(BF16)
        out_copy(0, h).start()
        out_copy(1, h).start()

        dort = dor_s[...].T
        for u in KEYS:
            f, l = SEEN[u]
            qcols = slice(f * B, (l + 1) * B)
            at = pl.ds(BASE[u] * B, (l + 1 - f) * B)
            dku = (dot_nn(qt[:, qcols], ds_s[at, :]) * math.log(2.0)).T
            dvu = dot_nn(dort[:, qcols], p_s[at, :]).T
            if u < 0:
                i = HALO_AT[u]
                gacc[1] += fold(dku * hn[i * B:(i + 1) * B])
                back[h, 0, pl.ds(i * B, B), :] = dku.astype(BF16)
                back[h, 1, pl.ds(i * B, B), :] = dvu.astype(BF16)
                if u == -1:
                    @pl.when(me > 0)
                    def _():
                        back_copy(h).start()
            else:
                raw = k_in[h, pl.ds(u * B, B), :].astype(F32)
                if u in TAIL:
                    i = TAIL.index(u)
                    unit = raw * lax.rsqrt(rowmean(raw * raw) + EPS)
                    tail_acc[h, 0, pl.ds(i * B, B), :] = dku
                    tail_acc[h, 1, pl.ds(i * B, B), :] = dvu
                else:
                    grad, unit = key_back(raw, dku)
                    dk_o[h, pl.ds(u * B, B), :] = grad.astype(BF16)
                    dv_o[h, pl.ds(u * B, B), :] = dvu.astype(BF16)
                gacc[1] += fold(dku * unit)

        @pl.when(h >= 2)
        def _():
            finish_tail(h - 2)

        return c

    lax.fori_loop(0, heads, head, 0)

    g1[me] = jnp.concatenate(
        [jnp.sum(gacc[i], axis=0, keepdims=True) for i in range(3)] + [jnp.zeros((5, D), F32)], axis=0)

    def c1(k):
        return pltpu.make_async_remote_copy(
            src_ref=g1.at[me], dst_ref=g1.at[me], send_sem=s1.at[k], recv_sem=r1.at[me],
            device_id={"ctx": lax.rem(me + k, n)}, device_id_type=MESH)

    def w1(k):
        src = lax.rem(me + n - k, n)
        return pltpu.make_async_remote_copy(
            src_ref=g1.at[src], dst_ref=g1.at[src], send_sem=s1.at[k], recv_sem=r1.at[src],
            device_id={"ctx": src}, device_id_type=MESH)

    def c2_(k):
        return pltpu.make_async_remote_copy(
            src_ref=g2.at[mf], dst_ref=g2.at[mf], send_sem=s2.at[k], recv_sem=r2.at[mf],
            device_id={"fsdp": lax.rem(mf + k, m)}, device_id_type=MESH)

    def w2(k):
        src = lax.rem(mf + m - k, m)
        return pltpu.make_async_remote_copy(
            src_ref=g2.at[src], dst_ref=g2.at[src], send_sem=s2.at[k], recv_sem=r2.at[src],
            device_id={"fsdp": src}, device_id_type=MESH)

    def loop(count, fn):
        def body(k, c):
            fn(k)
            return c

        lax.fori_loop(1, count, body, 0)

    loop(n, lambda k: c1(k).start())
    if heads >= 2:
        finish_tail(heads - 2)
    loop(n, lambda k: w1(k).wait_recv())
    g2[mf] = lax.fori_loop(0, n, lambda i, a: a + g1[i], jnp.zeros((8, D), F32))
    loop(m, lambda k: c2_(k).start())
    finish_tail(heads - 1)
    loop(m, lambda k: w2(k).wait_recv())
    total = lax.fori_loop(0, m, lambda i, a: a + g2[i], jnp.zeros((8, D), F32))
    gain_out[...] = total[0:3] * factor

    loop(n, lambda k: c1(k).wait_send())
    loop(m, lambda k: c2_(k).wait_send())

    def drain(h, c):
        for t in range(4):
            out_copy(t, h).wait()

        @pl.when(me < n - 1)
        def _():
            for piece in range(2):
                for kv in range(2):
                    halo_copy(h, kv, piece).wait_send()

        @pl.when(me > 0)
        def _():
            back_copy(h).wait_send()

        return c

    lax.fori_loop(0, heads, drain, 0)


def local(n, m, queries, key_input, value_input, out_grad, norm_gains, block_lists):
    rows, width = queries.shape
    heads = width // D
    factor = 1.0 / math.sqrt(rows * n * heads * m)
    hbm = pl.BlockSpec(memory_space=pl.ANY)
    vmem = pl.BlockSpec(memory_space=pltpu.VMEM)
    smem = pl.BlockSpec(memory_space=pltpu.SMEM)
    big = jax.ShapeDtypeStruct((rows, width), BF16)
    hrows = pltpu.VMEM((heads, rows, D), BF16)
    hhalo = pltpu.VMEM((heads, 2, 3 * B, D), BF16)
    dma = pltpu.SemaphoreType.DMA
    return pl.pallas_call(
        functools.partial(kernel, n, m, heads, factor),
        out_shape=[big, big, big, big, jax.ShapeDtypeStruct((3, D), F32)],
        in_specs=[hbm, hbm, hbm, hbm, vmem, smem],
        out_specs=[hbm, hbm, hbm, hbm, vmem],
        scratch_shapes=[
            hrows, hrows, hrows, hrows,
            hhalo, hhalo, hhalo,
            pltpu.VMEM((heads, 2, 3 * B, D), F32),
            hrows, hrows, hrows, hrows,
            pltpu.VMEM((PAIRS * B, B), BF16),
            pltpu.VMEM((PAIRS * B, B), BF16),
            pltpu.VMEM((rows, D), BF16),
            pltpu.VMEM((3, 8, D), F32),
            pltpu.VMEM((n, 8, D), F32),
            pltpu.VMEM((m, 8, D), F32),
            dma((4, heads)), dma((4, heads)),
            dma((heads, 2, 2)), dma((heads, 2, 2)),
            dma((heads,)), dma((heads,)),
            dma((n,)), dma((n,)), dma((m,)), dma((m,)),
        ],
        compiler_params=pltpu.CompilerParams(
            collective_id=0, has_side_effects=True, vmem_limit_bytes=48 * 1024 * 1024),
        cost_estimate=pl.CostEstimate(
            flops=heads * PAIRS * 12 * B * B * D, bytes_accessed=rows * width * 16,
            transcendentals=heads * PAIRS * B * B),
        name="block_sparse_attention",
    )(queries, key_input, value_input, out_grad, norm_gains, block_lists)


def solution(mesh):
    n = mesh.shape["ctx"]
    m = mesh.shape["fsdp"]
    spec = P("ctx", "fsdp")
    return jax.shard_map(
        functools.partial(local, n, m),
        mesh=mesh,
        in_specs=(spec, spec, spec, spec, P(), P("ctx", None)),
        out_specs=(spec, spec, spec, spec, P()),
        check_vma=False,
    )
```

profile of v0, /device:TPU:0, one launch (start us, length us, event | category | flops | bytes accessed | tf_op | source)
XLA Modules:
  0.0 57.4 jit_solution(6986922019921535996)
XLA Ops:
  0.6 0.0 copy-start
  0.6 1.3 %copy-done = bf16[768,768]{1,0:T(8,128)(2,1)S(1)} copy-done((bf16[768,768]{1,0:T(8,128)(2,1)S(1)}, bf16[768,768]{1,0:T(8,128)(2,1)}, u32[]{:S(2)}) %copy-start) | copy-done | bytes 1179672
  1.9 0.0 copy-start.1
  1.9 0.7 %copy-done.1 = s32[6,5]{1,0:T(8,128)S(1)} copy-done((s32[6,5]{1,0:T(8,128)S(1)}, s32[6,5]{1,0:T(8,128)}, u32[]{:S(2)}) %copy-start.1) | copy-done | bytes 144
  2.6 0.0 copy-start.2
  2.6 0.7 %copy-done.2 = f32[3,128]{1,0:T(4,128)S(1)} copy-done((f32[3,128]{1,0:T(4,128)S(1)}, f32[3,128]{1,0:T(4,128)}, u32[]{:S(2)}) %copy-start.2) | copy-done | bytes 1560
  3.3 49.5 %block_sparse_attention.1 = (bf16[768,768]{1,0:T(8,128)(2,1)S(1)}, bf16[768,768]{1,0:T(8,128)(2,1)S(1)}, bf16[768,768]{1,0:T(8,128)(2,1)S(1)}, bf16[768,768]{1,0:T(8,128)(2,1)S(1)}, f32[3,128]{1,0:T(4,128)S(1)}) custom-call(bf16[768,768]{1,0:T(8,128)(2,1)S(1)} %copy-done, bf16[768,768]{1,0:T(8,128)(2,1)} %k_hbm.1, bf16[768,768]{1,0:T(8,128)(2,1)} %v_hbm.1, ...), custom_call_target="tpu_custom_call" | custom-call | flops 3925868544 | bytes 9437184 | tf_op jit(solution)/shard_map/block_sparse_attention/pallas_call | solution.py:360
  52.8 1.0 %copy.16 = bf16[768,768]{1,0:T(8,128)(2,1)} copy(bf16[768,768]{1,0:T(8,128)(2,1)S(1)} %get-tuple-element.10) | data formatting | bytes 2359296
  53.8 1.0 %copy.17 = bf16[768,768]{1,0:T(8,128)(2,1)} copy(bf16[768,768]{1,0:T(8,128)(2,1)S(1)} %get-tuple-element.11) | data formatting | bytes 2359296
  54.8 1.0 %copy.18 = bf16[768,768]{1,0:T(8,128)(2,1)} copy(bf16[768,768]{1,0:T(8,128)(2,1)S(1)} %get-tuple-element.12) | data formatting | bytes 2359296
  55.8 1.0 %copy.19 = bf16[768,768]{1,0:T(8,128)(2,1)} copy(bf16[768,768]{1,0:T(8,128)(2,1)S(1)} %get-tuple-element.13) | data formatting | bytes 2359296
  56.8 0.6 %copy.20 = f32[3,128]{1,0:T(4,128)} copy(f32[3,128]{1,0:T(4,128)S(1)} %get-tuple-element.14) | data formatting | bytes 3072
Async XLA Ops:
  0.6 1.3 %copy-start = (bf16[768,768]{1,0:T(8,128)(2,1)S(1)}, bf16[768,768]{1,0:T(8,128)(2,1)}, u32[]{:S(2)}) copy-start(bf16[768,768]{1,0:T(8,128)(2,1)} %q_hbm.1) | copy-start | bytes 3538948
  1.9 0.7 %copy-start.1 = (s32[6,5]{1,0:T(8,128)S(1)}, s32[6,5]{1,0:T(8,128)}, u32[]{:S(2)}) copy-start(s32[6,5]{1,0:T(8,128)} %lists.1) | copy-start | bytes 364
  2.6 0.7 %copy-start.2 = (f32[3,128]{1,0:T(4,128)S(1)}, f32[3,128]{1,0:T(4,128)}, u32[]{:S(2)}) copy-start(f32[3,128]{1,0:T(4,128)} %gains.1) | copy-start | bytes 4612
where the time goes:
time: 57.6 us; the launch traced here: 57.4 us
  Pallas kernels  49.5 us (86%)
  local copies, waits for them, and re-layouts  7.26 us (13%)
  between operations  0.65 us (1%)
    pallas_call x1, Pallas kernels, local(): pl.pallas_call(functools.partial(kernel, n, m, heads, factor), out_shape=...  49.5 us
    unnamed x11, local copies, waits for them, and re-layouts  7.26 us

commit v1 on v0

--- a/solution.py
+++ b/solution.py
@@ -34,6 +34,7 @@
         WINDOW.append(((_far, 4), (_low, 2), (_b - 1, 1), (_b, 0)))
     else:
         WINDOW.append(((_far, 4), (_low, 3), (_b - 2, 2), (_b - 1, 1), (_b, 0)))
+ORDER = ((-2, -4, -1, 0, 1, 2), (1, -1, 2, 3, 4, 5))
 HALO_AT = {-4: 0, -2: 1, -1: 2}
 TAIL = (2, 4, 5)
 PIECES = ((2 * B, 0, B), (4 * B, B, 2 * B))
@@ -61,6 +62,7 @@
     att_hbm, dq_hbm, dk_hbm, dv_hbm, gain_out,
     q_in, k_in, v_in, do_in, halo, back, ret, tail_acc,
     att_o, dq_o, dk_o, dv_o, p_s, ds_s, dor_s, gacc, g1, g2,
+    nk_s, nq_s, rq_s, delta_s, hn_s, qs_s, qt_s, dort_s, kw, vw, ktw, vtw, pb_s, dsb_s,
     in_sem, out_sem, hs_sem, hr_sem, bs_sem, br_sem, s1, r1, s2, r2,
 ):
     me = lax.axis_index("ctx")
@@ -138,6 +140,7 @@
         ret[...] = jnp.zeros_like(ret)
 
     gacc[...] = jnp.zeros_like(gacc)
+    vw[:, :, D:] = jnp.ones((2, 6 * B, D), BF16)
     inv_root = 1.0 / math.sqrt(D)
     c2 = math.log2(math.e) * inv_root
     gq = gains[0:1, :]
@@ -174,12 +177,15 @@
         for t in range(4):
             in_copy(t, h).wait()
         kr = k_in[h].astype(F32)
-        kb = (kr * lax.rsqrt(rowmean(kr * kr) + EPS) * gk).astype(BF16)
+        nk_s[...] = kr * lax.rsqrt(rowmean(kr * kr) + EPS)
         qr = q_in[h].astype(F32)
         rq = lax.rsqrt(rowmean(qr * qr) + EPS)
-        qs = (qr * rq * gq2).astype(BF16)
-        qt = qs.T
-        vb = v_in[h]
+        nq = qr * rq
+        nq_s[...] = nq
+        rq_s[...] = jnp.broadcast_to(rq, nq.shape)
+        qs = (nq * gq2).astype(BF16)
+        qs_s[...] = qs
+        qt_s[...] = qs.T
 
         @pl.when(me > 0)
         def _():
@@ -188,90 +194,108 @@
                     halo_copy(h, kv, piece).wait_recv()
 
         hr = halo[h, 0].astype(F32)
-        hn = hr * lax.rsqrt(rowmean(hr * hr) + EPS)
-        hb = (hn * gk).astype(BF16)
-        hv = halo[h, 1]
-
-        def kblk(u):
-            return kb[u * B:(u + 1) * B] if u >= 0 else hb[HALO_AT[u] * B:(HALO_AT[u] + 1) * B]
-
-        def vblk(u):
-            return vb[u * B:(u + 1) * B] if u >= 0 else hv[HALO_AT[u] * B:(HALO_AT[u] + 1) * B]
-
-        ones = jnp.ones((B, D), BF16)
+        hn_s[...] = hr * lax.rsqrt(rowmean(hr * hr) + EPS)
+        for u in KEYS:
+            if u >= 0:
+                kb = (nk_s[pl.ds(u * B, B), :] * gk).astype(BF16)
+                vb = v_in[h, pl.ds(u * B, B), :]
+            else:
+                kb = (hn_s[pl.ds(HALO_AT[u] * B, B), :] * gk).astype(BF16)
+                vb = halo[h, 1, pl.ds(HALO_AT[u] * B, B), :]
+            kt = kb.T
+            vt = vb.T
+            for g in range(2):
+                if u in ORDER[g]:
+                    at = pl.ds(ORDER[g].index(u) * B, B)
+                    kw[g, at, :] = kb
+                    vw[g, at, 0:D] = vb
+                    ktw[g, :, at] = kt
+                    vtw[g, :, at] = vt
+
+        def window(b):
+            order = ORDER[b // 3]
+            return b // 3, order.index(WINDOW[b][0][0]) * B, len(WINDOW[b]) * B
+
         for b in range(6):
-            rows = slice(b * B, (b + 1) * B)
-            qb = qs[rows]
-            keys = jnp.concatenate([kblk(u) for u, _ in WINDOW[b]], axis=0)
-            vals = jnp.concatenate([vblk(u) for u, _ in WINDOW[b]], axis=0)
-            s = dot_nt(qb, keys)
-            ps = []
+            g, start, size = window(b)
+            s = dot_nn(qs_s[pl.ds(b * B, B), :], ktw[g, :, pl.ds(start, size)])
             for i, (u, slot) in enumerate(WINDOW[b]):
                 e = jnp.exp2(s[:, i * B:(i + 1) * B])
                 if slot == 0:
                     e = jnp.where(causal, e, 0.0)
                 else:
                     e = e * jnp.where(lists[b, slot] >= 0, 1.0, 0.0).astype(F32)
-                ps.append(e)
-            pb = jnp.concatenate([e.astype(BF16) for e in ps], axis=1)
-            vone = jnp.concatenate(
-                [vals, jnp.concatenate([ones] * len(ps), axis=0)], axis=1)
-            acc = dot_nn(pb, vone)
+                low = e.astype(BF16)
+                pb_s[b, :, pl.ds(i * B, B)] = low
+                p_s[pl.ds((BASE[u] + b - SEEN[u][0]) * B, B), :] = low
+
+        dout_sum = jnp.zeros((8, D), F32)
+        for b in range(6):
+            g, start, size = window(b)
+            acc = dot_nn(pb_s[b, :, pl.ds(0, size)], vw[g, pl.ds(start, size), :])
             r = 1.0 / acc[:, D:]
             out = acc[:, :D] * r
             att_o[h, pl.ds(b * B, B), :] = (out * go).astype(BF16)
             dout = do_in[h, pl.ds(b * B, B), :].astype(F32)
-            gacc[2] += fold(dout * out)
+            dout_sum += fold(dout * out)
             dor = (dout * go * r).astype(BF16)
             dor_s[pl.ds(b * B, B), :] = dor
+            dort_s[:, pl.ds(b * B, B)] = dor.T
             delta = jnp.sum(dor.astype(F32) * out, axis=-1, keepdims=True)
-            dp = dot_nt(dor, vals)
-            dss = []
+            delta_s[pl.ds(b * B, B), :] = jnp.broadcast_to(delta, out.shape)
+        gacc[2] += dout_sum
+        out_copy(0, h).start()
+
+        for b in range(6):
+            g, start, size = window(b)
+            dp = dot_nn(dor_s[pl.ds(b * B, B), :], vtw[g, :, pl.ds(start, size)])
+            delta = delta_s[pl.ds(b * B, B), :]
             for i, (u, slot) in enumerate(WINDOW[b]):
-                ds = (ps[i] * (dp[:, i * B:(i + 1) * B] - delta)).astype(BF16)
-                dss.append(ds)
-                at = pl.ds((BASE[u] + b - SEEN[u][0]) * B, B)
-                p_s[at, :] = pb[:, i * B:(i + 1) * B]
-                ds_s[at, :] = ds
-            dqn = dot_nn(jnp.concatenate(dss, axis=1), keys) * inv_root
-            raw = qr[rows]
-            scale = rq[rows]
-            unit = raw * scale
-            gacc[0] += fold(dqn * unit)
-            inner = dqn * gq
-            grad = scale * (inner - unit * rowmean(inner * unit))
-            dq_o[h, pl.ds(b * B, B), :] = grad.astype(BF16)
-        out_copy(0, h).start()
-        out_copy(1, h).start()
-
-        dort = dor_s[...].T
+                p = pb_s[b, :, pl.ds(i * B, B)].astype(F32)
+                ds = (p * (dp[:, i * B:(i + 1) * B] - delta)).astype(BF16)
+                dsb_s[b, :, pl.ds(i * B, B)] = ds
+                ds_s[pl.ds((BASE[u] + b - SEEN[u][0]) * B, B), :] = ds
+
+        key_sum = jnp.zeros((8, D), F32)
         for u in KEYS:
             f, l = SEEN[u]
-            qcols = slice(f * B, (l + 1) * B)
+            qcols = pl.ds(f * B, (l + 1 - f) * B)
             at = pl.ds(BASE[u] * B, (l + 1 - f) * B)
-            dku = (dot_nn(qt[:, qcols], ds_s[at, :]) * math.log(2.0)).T
-            dvu = dot_nn(dort[:, qcols], p_s[at, :]).T
+            dku = (dot_nn(qt_s[:, qcols], ds_s[at, :]) * math.log(2.0)).T
+            dvu = dot_nn(dort_s[:, qcols], p_s[at, :]).astype(BF16).T
             if u < 0:
                 i = HALO_AT[u]
-                gacc[1] += fold(dku * hn[i * B:(i + 1) * B])
+                key_sum += fold(dku * hn_s[pl.ds(i * B, B), :])
                 back[h, 0, pl.ds(i * B, B), :] = dku.astype(BF16)
-                back[h, 1, pl.ds(i * B, B), :] = dvu.astype(BF16)
+                back[h, 1, pl.ds(i * B, B), :] = dvu
                 if u == -1:
                     @pl.when(me > 0)
                     def _():
                         back_copy(h).start()
             else:
-                raw = k_in[h, pl.ds(u * B, B), :].astype(F32)
+                key_sum += fold(dku * nk_s[pl.ds(u * B, B), :])
                 if u in TAIL:
                     i = TAIL.index(u)
-                    unit = raw * lax.rsqrt(rowmean(raw * raw) + EPS)
                     tail_acc[h, 0, pl.ds(i * B, B), :] = dku
-                    tail_acc[h, 1, pl.ds(i * B, B), :] = dvu
+                    tail_acc[h, 1, pl.ds(i * B, B), :] = dvu.astype(F32)
                 else:
-                    grad, unit = key_back(raw, dku)
+                    grad, unit = key_back(k_in[h, pl.ds(u * B, B), :].astype(F32), dku)
                     dk_o[h, pl.ds(u * B, B), :] = grad.astype(BF16)
-                    dv_o[h, pl.ds(u * B, B), :] = dvu.astype(BF16)
-                gacc[1] += fold(dku * unit)
+                    dv_o[h, pl.ds(u * B, B), :] = dvu
+        gacc[1] += key_sum
+
+        query_sum = jnp.zeros((8, D), F32)
+        for b in range(6):
+            g, start, size = window(b)
+            rows = pl.ds(b * B, B)
+            dqn = dot_nn(dsb_s[b, :, pl.ds(0, size)], kw[g, pl.ds(start, size), :]) * inv_root
+            unit = nq_s[rows, :]
+            query_sum += fold(dqn * unit)
+            inner = dqn * gq
+            grad = rq_s[rows, :] * (inner - unit * rowmean(inner * unit))
+            dq_o[h, rows, :] = grad.astype(BF16)
+        gacc[0] += query_sum
+        out_copy(1, h).start()
 
         @pl.when(h >= 2)
         def _():
@@ -356,6 +380,7 @@
     big = jax.ShapeDtypeStruct((rows, width), BF16)
     hrows = pltpu.VMEM((heads, rows, D), BF16)
     hhalo = pltpu.VMEM((heads, 2, 3 * B, D), BF16)
+    frows = pltpu.VMEM((rows, D), F32)
     dma = pltpu.SemaphoreType.DMA
     return pl.pallas_call(
         functools.partial(kernel, n, m, heads, factor),
@@ -373,13 +398,24 @@
             pltpu.VMEM((3, 8, D), F32),
             pltpu.VMEM((n, 8, D), F32),
             pltpu.VMEM((m, 8, D), F32),
+            frows, frows, frows, frows,
+            pltpu.VMEM((3 * B, D), F32),
+            pltpu.VMEM((rows, D), BF16),
+            pltpu.VMEM((D, rows), BF16),
+            pltpu.VMEM((D, rows), BF16),
+            pltpu.VMEM((2, 6 * B, D), BF16),
+            pltpu.VMEM((2, 6 * B, 2 * D), BF16),
+            pltpu.VMEM((2, D, 6 * B), BF16),
+            pltpu.VMEM((2, D, 6 * B), BF16),
+            pltpu.VMEM((6, B, 5 * B), BF16),
+            pltpu.VMEM((6, B, 5 * B), BF16),
             dma((4, heads)), dma((4, heads)),
             dma((heads, 2, 2)), dma((heads, 2, 2)),
             dma((heads,)), dma((heads,)),
             dma((n,)), dma((n,)), dma((m,)), dma((m,)),
         ],
         compiler_params=pltpu.CompilerParams(
-            collective_id=0, has_side_effects=True, vmem_limit_bytes=48 * 1024 * 1024),
+            collective_id=0, has_side_effects=True, vmem_limit_bytes=60 * 1024 * 1024),
         cost_estimate=pl.CostEstimate(
             flops=heads * PAIRS * 12 * B * B * D, bytes_accessed=rows * width * 16,
             transcendentals=heads * PAIRS * B * B),

time: 57.6 us -> 47.8 us (0.83)
  Pallas kernels: 49.5 us -> 39.4 us
    pallas_call x1, Pallas kernels: 49.5 us -> 39.4 us  [local(): pl.pallas_call(functools.partial(kernel, n, m, heads, factor), out_shape=...]
    unnamed x11 -> x13, local copies, waits for them, and re-layouts: 7.26 us -> 7.44 us
where the time goes in v1:
time: 47.8 us; the launch traced here: 47.5 us
  Pallas kernels  39.4 us (82%)
  local copies, waits for them, and re-layouts  7.44 us (16%)
  between operations  0.65 us (1%)
    pallas_call x1, Pallas kernels, local(): pl.pallas_call(functools.partial(kernel, n, m, heads, factor), out_shape=...  39.4 us
    unnamed x13, local copies, waits for them, and re-layouts  7.44 us

profile of v1, /device:TPU:0, one launch (start us, length us, event | category | flops | bytes accessed | tf_op | source)
XLA Modules:
  0.0 47.5 jit_solution(13220291682731588706)
XLA Ops:
  0.6 39.4 %block_sparse_attention.1 = (bf16[768,768]{1,0:T(8,128)(2,1)}, bf16[768,768]{1,0:T(8,128)(2,1)}, bf16[768,768]{1,0:T(8,128)(2,1)}, bf16[768,768]{1,0:T(8,128)(2,1)}, f32[3,128]{1,0:T(4,128)}) custom-call(bf16[768,768]{1,0:T(8,128)(2,1)} %q_hbm.1, bf16[768,768]{1,0:T(8,128)(2,1)} %k_hbm.1, bf16[768,768]{1,0:T(8,128)(2,1)} %v_hbm.1, bf16[768,768]{1,0:T(8,128)(2,1)} %do_hbm.1, ...), custom_call_target="tpu_custom_call" | custom-call | flops 3925868544 | bytes 9437184 | tf_op jit(solution)/shard_map/block_sparse_attention/pallas_call | solution.py:385
  40.1 0.0 copy-start.2
  40.1 2.5 %copy.16 = bf16[768,768]{1,0:T(8,128)(2,1)} copy(bf16[768,768]{1,0:T(8,128)(2,1)} %get-tuple-element.10) | data formatting | bytes 2359296
  42.5 0.0 copy-done.2
  42.5 0.0 copy-start.1
  42.5 1.0 %copy.17 = bf16[768,768]{1,0:T(8,128)(2,1)} copy(bf16[768,768]{1,0:T(8,128)(2,1)S(1)} %copy-done.2) | data formatting | bytes 2359296
  43.5 0.7 %copy-done.1 = bf16[768,768]{1,0:T(8,128)(2,1)S(1)} copy-done((bf16[768,768]{1,0:T(8,128)(2,1)S(1)}, bf16[768,768]{1,0:T(8,128)(2,1)}, u32[]{:S(2)}) %copy-start.1) | copy-done | bytes 1179672
  44.2 0.0 copy-start
  44.2 1.0 %copy.18 = bf16[768,768]{1,0:T(8,128)(2,1)} copy(bf16[768,768]{1,0:T(8,128)(2,1)S(1)} %copy-done.1) | data formatting | bytes 2359296
  45.2 0.7 %copy-done = bf16[768,768]{1,0:T(8,128)(2,1)S(1)} copy-done((bf16[768,768]{1,0:T(8,128)(2,1)S(1)}, bf16[768,768]{1,0:T(8,128)(2,1)}, u32[]{:S(2)}) %copy-start) | copy-done | bytes 1179672
  45.9 0.0 copy-start.3
  45.9 1.0 %copy.19 = bf16[768,768]{1,0:T(8,128)(2,1)} copy(bf16[768,768]{1,0:T(8,128)(2,1)S(1)} %copy-done) | data formatting | bytes 2359296
  46.9 0.0 copy-done.3
  46.9 0.6 %copy.20 = f32[3,128]{1,0:T(4,128)} copy(f32[3,128]{1,0:T(4,128)S(1)} %copy-done.3) | data formatting | bytes 3072
Async XLA Ops:
  40.1 2.5 %copy-start.2 = (bf16[768,768]{1,0:T(8,128)(2,1)S(1)}, bf16[768,768]{1,0:T(8,128)(2,1)}, u32[]{:S(2)}) copy-start(bf16[768,768]{1,0:T(8,128)(2,1)} %get-tuple-element.11) | copy-start | bytes 3538948
  42.5 1.7 %copy-start.1 = (bf16[768,768]{1,0:T(8,128)(2,1)S(1)}, bf16[768,768]{1,0:T(8,128)(2,1)}, u32[]{:S(2)}) copy-start(bf16[768,768]{1,0:T(8,128)(2,1)} %get-tuple-element.12) | copy-start | bytes 3538948
  44.2 1.7 %copy-start = (bf16[768,768]{1,0:T(8,128)(2,1)S(1)}, bf16[768,768]{1,0:T(8,128)(2,1)}, u32[]{:S(2)}) copy-start(bf16[768,768]{1,0:T(8,128)(2,1)} %get-tuple-element.13) | copy-start | bytes 3538948
  45.9 1.0 %copy-start.3 = (f32[3,128]{1,0:T(4,128)S(1)}, f32[3,128]{1,0:T(4,128)}, u32[]{:S(2)}) copy-start(f32[3,128]{1,0:T(4,128)} %get-tuple-element.14) | copy-start | bytes 4612
